TPU v7x, 128 devices: a whole 4x4x4 slice. The times are simulated.
128 devices in a mesh: grp: 4 (over y), own: 32 (over x, z, core).
Axes of the slice: x: 4, y: 4, z: 4, core: 2. Of those that a mesh axis runs over, the one named last changes fastest.
Arguments:
- user_slot: int32 [4, 128, 128], P(None, ('grp', 'own')), may hold values from 0 to 127, each once within a row
- item_slot: int32 [4, 128, 128], P(None, ('grp', 'own')), may hold values from 0 to 127, each once within a row
- block_counts: int32 [4, 128, 128], P(None, ('grp', 'own')), may hold values from 0 to 1, as said below
- time_gaps: float32 [4, 16384], P(None, ('grp', 'own')), may hold values from -4 to 4
- user_prev: bfloat16 [4, 16384, 512], P(None, ('grp', 'own')), may hold values from -1 to 1
- item_prev: bfloat16 [4, 16384, 512], P(None, ('grp', 'own')), may hold values from -1 to 1
- user_cotangent: float32 [16384, 512], P(('grp', 'own')), may hold values from -6 to 6
- item_cotangent: float32 [16384, 512], P(('grp', 'own')), may hold values from -6 to 6
- user_weight: bfloat16 [1024, 512], replicated, may hold values from -0.1875 to 0.1875
- item_weight: bfloat16 [1024, 512], replicated, may hold values from -0.1875 to 0.1875
- bias_time: float32 [4, 512], replicated, may hold values from -3 to 3
Outputs:
- user_adjoint: float32 [16384, 512], P(('grp', 'own'))
- item_adjoint: float32 [16384, 512], P(('grp', 'own'))
- weight_grads: float32 [2048, 512], P(('grp', 'own'))
- vector_grads: float32 [4, 512], replicated
Inputs may be any that keep to these rules, and one draw needn't show every extreme that they name: `user_slot`: each [b, s] row is a permutation, padded rows included. `item_slot`: each [b, p] row is a permutation, padded rows included. block_counts[b, s, p] is the number of live rows from user owner s to item owner p; in every t-batch some item owner receives 1 row from every user owner.
All inputs are finite; a program needn't handle non-finite values.
Results may differ from a plain program's by a relative error of at most 0.0034.
Values sent between devices are 32-bit elements; how exact they have to be, the bound alone decides.
A program may use at most 128 MiB of HBM per device.

v0:
```python
import math

import jax
import jax.numpy as jnp
from jax import lax
from jax.sharding import PartitionSpec as P


def backward_rows(
    user_rows,
    item_rows,
    gap_rows,
    live_rows,
    grad_user,
    grad_item,
    user_weight,
    item_weight,
    bias_time,
):
    features = user_rows.shape[-1]
    pre_user = (
        jnp.dot(user_rows, user_weight[:features], preferred_element_type=jnp.float32)
        + jnp.dot(item_rows, user_weight[features:], preferred_element_type=jnp.float32)
        + gap_rows[:, None] * bias_time[1]
        + bias_time[0]
    )
    pre_item = (
        jnp.dot(item_rows, item_weight[:features], preferred_element_type=jnp.float32)
        + jnp.dot(user_rows, item_weight[features:], preferred_element_type=jnp.float32)
        + gap_rows[:, None] * bias_time[3]
        + bias_time[2]
    )
    state_user = jnp.tanh(pre_user)
    state_item = jnp.tanh(pre_item)
    live_mask = live_rows.astype(jnp.float32)[:, None]
    delta_user = live_mask * grad_user * (1.0 - state_user * state_user)
    delta_item = live_mask * grad_item * (1.0 - state_item * state_item)
    low_user = delta_user.astype(jnp.bfloat16)
    low_item = delta_item.astype(jnp.bfloat16)
    new_user = jnp.dot(
        low_user, user_weight[:features].T, preferred_element_type=jnp.float32
    ) + jnp.dot(low_item, item_weight[features:].T, preferred_element_type=jnp.float32)
    new_item = jnp.dot(
        low_user, user_weight[features:].T, preferred_element_type=jnp.float32
    ) + jnp.dot(low_item, item_weight[:features].T, preferred_element_type=jnp.float32)
    weight_terms = jnp.concatenate(
        [
            jnp.dot(user_rows.T, low_user, preferred_element_type=jnp.float32),
            jnp.dot(item_rows.T, low_user, preferred_element_type=jnp.float32),
            jnp.dot(item_rows.T, low_item, preferred_element_type=jnp.float32),
            jnp.dot(user_rows.T, low_item, preferred_element_type=jnp.float32),
        ],
        axis=0,
    )
    vector_terms = jnp.stack(
        [
            jnp.sum(delta_user, axis=0),
            jnp.sum(gap_rows[:, None] * delta_user, axis=0),
            jnp.sum(delta_item, axis=0),
            jnp.sum(gap_rows[:, None] * delta_item, axis=0),
        ],
        axis=0,
    )
    return (new_user, new_item, weight_terms, vector_terms)


def send_request(rows_in):
    result = lax.all_to_all(rows_in, ("grp", "own"), split_axis=0, concat_axis=0, tiled=True)
    return result


def send_return(rows_in):
    result = lax.all_to_all(rows_in, ("grp", "own"), split_axis=0, concat_axis=0, tiled=True)
    return result


def per_device(
    user_slot,
    item_slot,
    block_counts,
    time_gaps,
    user_prev,
    item_prev,
    user_cotangent,
    item_cotangent,
    user_weight,
    item_weight,
    bias_time,
):
    groups = lax.axis_size("grp")
    members = lax.axis_size("own")
    owners = groups * members
    batches = user_slot.shape[0]
    row_count = user_slot.shape[-1]
    capacity = row_count // owners
    features = user_prev.shape[-1]
    grad_scale = 1.0 / math.sqrt(batches * owners * row_count)
    slot_users = user_slot.reshape(batches, row_count)
    slot_items = item_slot.reshape(batches, row_count)
    sent_counts = block_counts.reshape(batches, owners)
    got_counts = lax.all_to_all(
        sent_counts, ("grp", "own"), split_axis=1, concat_axis=1, tiled=True
    )
    positions = jnp.arange(capacity, dtype=jnp.int32)
    live_sent = (positions[None, None, :] < sent_counts[:, :, None]).reshape(batches, row_count)
    live_got = (positions[None, None, :] < got_counts[:, :, None]).reshape(batches, row_count)
    adj_users = user_cotangent
    adj_items = item_cotangent
    weight_total = jnp.zeros((4 * features, features), jnp.float32)
    vector_total = jnp.zeros((4, features), jnp.float32)
    for position in range(batches - 1, -1, -1):
        requested = adj_items[slot_items[position]]
        arrived = send_request(requested)
        grad_user = adj_users[slot_users[position]]
        new_user, new_item, weight_terms, vector_terms = backward_rows(
            user_prev[position],
            item_prev[position],
            time_gaps[position],
            live_sent[position],
            grad_user,
            arrived,
            user_weight,
            item_weight,
            bias_time,
        )
        returned = send_return(new_item)
        weight_total = weight_total + weight_terms
        vector_total = vector_total + vector_terms
        adj_users = adj_users.at[slot_users[position]].set(
            jnp.where(live_sent[position][:, None], new_user, grad_user)
        )
        adj_items = adj_items.at[slot_items[position]].set(
            jnp.where(live_got[position][:, None], returned, requested)
        )
    weight_share = lax.psum_scatter(weight_total, ("grp", "own"), scatter_dimension=0, tiled=True)
    vector_whole = lax.psum(vector_total, ("grp", "own"))
    return (adj_users, adj_items, weight_share * grad_scale, vector_whole * grad_scale)


def solution(mesh):
    in_specs = (
        P(None, ("grp", "own"), None),
        P(None, ("grp", "own"), None),
        P(None, ("grp", "own"), None),
        P(None, ("grp", "own")),
        P(None, ("grp", "own"), None),
        P(None, ("grp", "own"), None),
        P(("grp", "own"), None),
        P(("grp", "own"), None),
        P(),
        P(),
        P(),
    )
    out_specs = (P(("grp", "own"), None), P(("grp", "own"), None), P(("grp", "own"), None), P())
    return jax.shard_map(
        per_device, mesh=mesh, in_specs=in_specs, out_specs=out_specs, check_vma=False
    )
```

profile of v0, /device:TPU:0, one launch (start us, length us, event | category | flops | bytes accessed | tf_op | source)
XLA Modules:
  0.0 883.1 jit_solution(1097821290479909339)
XLA Ops:
  10.7 11.1 %all-to-all-start.1 = ((s32[4,128,1]{0,2,1:T(1,128)}), s32[4,128,1]{0,2,1:T(1,128)S(1)}, u32[]{:S(2)}, u32[]{:S(2)}) async-start(s32[4,128,1]{0,2,1:T(1,128)} %bitcast.2), calls=%async_computation.1 | async-start | bytes 131072 | tf_op jit(solution)/shard_map/all_to_all | solution.py:101
  22.9 2.1 fusion.94
  24.9 2.1 fusion.104
  27.0 2.1 fusion.74
  30.0 1.8 fusion.98
  37.3 9.6 %slice_reduce_fusion.2 = (pred[128]{0:T(512)(128)(4,1)S(1)}, pred[128]{0:T(512)(128)(4,1)S(1)}, pred[128]{0:T(512)(128)(4,1)S(1)}, pred[128]{0:T(512)(128)(4,1)S(1)}) fusion(pred[4,128,1]{0,2,1:T(4,128)(4,1)S(1)} %broadcast_compare_fusion.1), kind=kLoop, calls=%fused_computation.133 | loop fusion | bytes 1024 | tf_op jit(solution)/shard_map/slice | solution.py:130
  51.9 10.8 %all-to-all-start = ((f32[128,1,512]{2,1,0:T(1,128)}), f32[128,1,512]{2,1,0:T(1,128)}, u32[]{:S(2)}, u32[]{:S(2)}) async-start(f32[128,1,512]{2,1,0:T(1,128)} %copy.25), calls=%async_computation | async-start | bytes 524288 | tf_op jit(solution)/shard_map/all_to_all | solution.py:68
  62.8 10.2 %slice_reduce_fusion = (pred[128]{0:T(512)(128)(4,1)}, pred[128]{0:T(512)(128)(4,1)}, pred[128]{0:T(512)(128)(4,1)}, pred[128]{0:T(512)(128)(4,1)}) fusion(pred[4,128,1]{0,2,1:T(4,128)(4,1)S(1)} %broadcast_compare_fusion), kind=kLoop, calls=%fused_computation.131 | loop fusion | bytes 1024 | tf_op jit(solution)/shard_map/slice | solution.py:133
  74.6 2.0 fusion.198
  77.9 2.2 convolution_bitcast_fusion.14
  82.8 10.2 %all-to-all-start.2 = ((f32[128,1,512]{2,1,0:T(1,128)}), f32[128,1,512]{2,1,0:T(1,128)}, u32[]{:S(2)}, u32[]{:S(2)}) async-start(f32[128,1,512]{2,1,0:T(1,128)} %copy.26), calls=%async_computation.2 | async-start | bytes 524288 | tf_op jit(solution)/shard_map/all_to_all | solution.py:73
  93.0 2.0 fusion.8
  95.1 8.3 all-to-all-done.2
  103.4 1.6 scatter_custom_fusion.1
  106.9 5.9 all-to-all-start.3
  114.1 1.5 scatter_fusion
  115.7 1.6 gather_fusion.2
  117.3 2.2 convolution_bitcast_fusion.13
  119.5 3.7 all-to-all-done.3
  124.5 2.0 fusion.196
  127.8 2.2 convolution_bitcast_fusion.10
  132.7 6.6 all-to-all-start.4
  139.2 2.0 fusion.11
  141.3 8.5 all-to-all-done.4
  149.7 1.6 scatter_custom_fusion.3
  153.1 5.7 all-to-all-start.5
  160.2 1.5 scatter_fusion.1
  163.2 2.2 convolution_bitcast_fusion.9
  165.4 3.9 all-to-all-done.5
  170.7 2.0 fusion.194
  174.0 2.3 convolution_bitcast_fusion.6
  179.0 6.3 all-to-all-start.6
  185.3 2.0 fusion.14
  187.4 8.4 all-to-all-done.6
  195.8 1.6 scatter_custom_fusion.5
  199.2 5.7 all-to-all-start.7
  206.3 1.8 scatter_fusion.2
  209.5 2.2 convolution_bitcast_fusion.5
  211.7 3.7 all-to-all-done.7
  215.5 1.5 fusion.22
  216.9 2.0 fusion.192
  218.9 2.3 convolution_bitcast_fusion.2
  223.9 2.2 convolution_bitcast_fusion.1
  226.2 6.2 fusion.1
  234.5 6.5 all-to-all-start.8
  243.1 67.9 %psum.7 = f32[4,512]{1,0:T(4,128)S(1)} all-reduce(f32[4,512]{1,0:T(4,128)S(1)} %fusion.183), channel_id=1, replica_groups=mesh['grp'=4,'own'=32] {'grp','own'}, use_global_device_ids=true, to_apply=%region_25.26 | all-reduce | flops 2048 | bytes 16384 | tf_op jit(solution)/shard_map/psum | solution.py:136
  311.6 1.6 scatter_custom_fusion.7
  313.2 561.4 %reduce-scatter.2.cloned.1.call-done = f32[16,512]{1,0:T(8,128)} async-done(((f32[2048,512]{1,0:T(8,128)}), f32[16,512]{1,0:T(8,128)}) %reduce-scatter.2.cloned.1.call-update) | async-done | bytes 32784 | tf_op jit(solution)/shard_map/reduce_scatter | solution.py:135
  (183 shorter events, 52.7 us)
Async XLA Ops:
  7.2 21.9 %copy-start.4 = (bf16[4,128,512]{2,1,0:T(8,128)(2,1)S(1)}, bf16[4,128,512]{2,1,0:T(8,128)(2,1)}, u32[]{:S(2)}) copy-start(bf16[4,128,512]{2,1,0:T(8,128)(2,1)} %param.15) | copy-start | bytes 1572868
  7.2 21.9 %copy-start.2 = (bf16[1024,512]{1,0:T(8,128)(2,1)S(1)}, bf16[1024,512]{1,0:T(8,128)(2,1)}, u32[]{:S(2)}) copy-start(bf16[1024,512]{1,0:T(8,128)(2,1)} %param.19) | copy-start | bytes 3145732
  7.2 22.8 %copy-start.3 = (bf16[1024,512]{1,0:T(8,128)(2,1)S(1)}, bf16[1024,512]{1,0:T(8,128)(2,1)}, u32[]{:S(2)}) copy-start(bf16[1024,512]{1,0:T(8,128)(2,1)} %param.20) | copy-start | bytes 3145732
  8.3 26.4 %copy-start.40 = (s32[4,1,128]{2,1,0:T(1,128)S(1)}, s32[4,1,128]{2,1,0:T(1,128)}, u32[]{:S(2)}) copy-start(s32[4,1,128]{2,1,0:T(1,128)} %param.11) | copy-start | bytes 6148
  8.3 26.4 %copy-start.41 = (s32[4,1,128]{2,1,0:T(1,128)S(1)}, s32[4,1,128]{2,1,0:T(1,128)}, u32[]{:S(2)}) copy-start(s32[4,1,128]{2,1,0:T(1,128)} %param.12) | copy-start | bytes 6148
  8.3 26.4 %copy-start.42 = (f32[4,128]{1,0:T(4,128)S(1)}, f32[4,128]{1,0:T(4,128)}, u32[]{:S(2)}) copy-start(f32[4,128]{1,0:T(4,128)} %param.14) | copy-start | bytes 6148
  8.3 28.4 %copy-start.15 = (f32[4,512]{1,0:T(4,128)S(1)}, f32[4,512]{1,0:T(4,128)}, u32[]{:S(2)}) copy-start(f32[4,512]{1,0:T(4,128)} %param.21) | copy-start | bytes 24580
  10.7 41.2 %all-to-all-start.1 = ((s32[4,128,1]{0,2,1:T(1,128)}), s32[4,128,1]{0,2,1:T(1,128)S(1)}, u32[]{:S(2)}, u32[]{:S(2)}) async-start(s32[4,128,1]{0,2,1:T(1,128)} %bitcast.2), calls=%async_computation.1 | async-start | bytes 131072 | tf_op jit(solution)/shard_map/all_to_all | solution.py:101
  21.9 10.0 %copy-start.5 = (bf16[4,128,512]{2,1,0:T(8,128)(2,1)S(1)}, bf16[4,128,512]{2,1,0:T(8,128)(2,1)}, u32[]{:S(2)}) copy-start(bf16[4,128,512]{2,1,0:T(8,128)(2,1)} %param.16) | copy-start | bytes 1572868
  34.7 39.8 %copy-start.18 = (s32[128]{0:T(128)}, s32[128]{0:T(128)S(1)}, u32[]{:S(2)}) copy-start(s32[128]{0:T(128)S(1)} %get-tuple-element.51) | copy-start | bytes 1540
  34.7 39.8 %copy-start.20 = (s32[128]{0:T(128)}, s32[128]{0:T(128)S(1)}, u32[]{:S(2)}) copy-start(s32[128]{0:T(128)S(1)} %get-tuple-element.49) | copy-start | bytes 1540
  34.7 39.8 %copy-start.21 = (s32[128]{0:T(128)}, s32[128]{0:T(128)S(1)}, u32[]{:S(2)}) copy-start(s32[128]{0:T(128)S(1)} %get-tuple-element.50) | copy-start | bytes 1540
  35.4 39.1 %copy-start.53 = (f32[128]{0:T(128)}, f32[128]{0:T(128)S(1)}, u32[]{:S(2)}) copy-start(f32[128]{0:T(128)S(1)} %get-tuple-element.46) | copy-start | bytes 1540
  37.3 37.2 %copy-start.48 = (f32[1,512]{1,0:T(1,128)}, f32[1,512]{1,0:T(1,128)S(1)}, u32[]{:S(2)}) copy-start(f32[1,512]{1,0:T(1,128)S(1)} %get-tuple-element.36) | copy-start | bytes 6148
  37.3 37.2 %copy-start.50 = (f32[1,512]{1,0:T(1,128)}, f32[1,512]{1,0:T(1,128)S(1)}, u32[]{:S(2)}) copy-start(f32[1,512]{1,0:T(1,128)S(1)} %get-tuple-element.39) | copy-start | bytes 6148
  46.9 27.6 %copy-start.22 = (pred[128]{0:T(512)(128)(4,1)}, pred[128]{0:T(512)(128)(4,1)S(1)}, u32[]{:S(2)}) copy-start(pred[128]{0:T(512)(128)(4,1)S(1)} %get-tuple-element.24) | copy-start | bytes 388
  46.9 27.6 %copy-start.24 = (pred[128]{0:T(512)(128)(4,1)}, pred[128]{0:T(512)(128)(4,1)S(1)}, u32[]{:S(2)}) copy-start(pred[128]{0:T(512)(128)(4,1)S(1)} %get-tuple-element.25) | copy-start | bytes 388
  46.9 27.6 %copy-start.26 = (pred[128]{0:T(512)(128)(4,1)}, pred[128]{0:T(512)(128)(4,1)S(1)}, u32[]{:S(2)}) copy-start(pred[128]{0:T(512)(128)(4,1)S(1)} %get-tuple-element.26) | copy-start | bytes 388
  46.9 27.6 %copy-start.27 = (pred[128]{0:T(512)(128)(4,1)}, pred[128]{0:T(512)(128)(4,1)S(1)}, u32[]{:S(2)}) copy-start(pred[128]{0:T(512)(128)(4,1)S(1)} %get-tuple-element.27) | copy-start | bytes 388
  48.7 25.8 %copy-start.54 = (f32[128]{0:T(128)}, f32[128]{0:T(128)S(1)}, u32[]{:S(2)}) copy-start(f32[128]{0:T(128)S(1)} %convert_element_type.52) | copy-start | bytes 1540
  51.9 21.2 %all-to-all-start = ((f32[128,1,512]{2,1,0:T(1,128)}), f32[128,1,512]{2,1,0:T(1,128)}, u32[]{:S(2)}, u32[]{:S(2)}) async-start(f32[128,1,512]{2,1,0:T(1,128)} %copy.25), calls=%async_computation | async-start | bytes 524288 | tf_op jit(solution)/shard_map/all_to_all | solution.py:68
  82.8 20.5 %all-to-all-start.2 = ((f32[128,1,512]{2,1,0:T(1,128)}), f32[128,1,512]{2,1,0:T(1,128)}, u32[]{:S(2)}, u32[]{:S(2)}) async-start(f32[128,1,512]{2,1,0:T(1,128)} %copy.26), calls=%async_computation.2 | async-start | bytes 524288 | tf_op jit(solution)/shard_map/all_to_all | solution.py:73
  106.9 16.3 %all-to-all-start.3 = ((f32[128,1,512]{2,1,0:T(1,128)}), f32[128,1,512]{2,1,0:T(1,128)}, u32[]{:S(2)}, u32[]{:S(2)}) async-start(f32[128,1,512]{2,1,0:T(1,128)} %copy.27), calls=%async_computation.3 | async-start | bytes 524288 | tf_op jit(solution)/shard_map/all_to_all | solution.py:68
  132.7 17.1 %all-to-all-start.4 = ((f32[128,1,512]{2,1,0:T(1,128)}), f32[128,1,512]{2,1,0:T(1,128)}, u32[]{:S(2)}, u32[]{:S(2)}) async-start(f32[128,1,512]{2,1,0:T(1,128)} %copy.28), calls=%async_computation.4 | async-start | bytes 524288 | tf_op jit(solution)/shard_map/all_to_all | solution.py:73
  153.1 16.2 %all-to-all-start.5 = ((f32[128,1,512]{2,1,0:T(1,128)}), f32[128,1,512]{2,1,0:T(1,128)}, u32[]{:S(2)}, u32[]{:S(2)}) async-start(f32[128,1,512]{2,1,0:T(1,128)} %copy.29), calls=%async_computation.5 | async-start | bytes 524288 | tf_op jit(solution)/shard_map/all_to_all | solution.py:68
  160.2 10.5 %copy-start.47 = (f32[1,512]{1,0:T(1,128)S(1)}, f32[1,512]{1,0:T(1,128)}, u32[]{:S(2)}) copy-start(f32[1,512]{1,0:T(1,128)} %get-tuple-element.37) | copy-start | bytes 6148
  170.7 14.6 %copy-start.25 = (pred[128]{0:T(512)(128)(4,1)S(1)}, pred[128]{0:T(512)(128)(4,1)}, u32[]{:S(2)}) copy-start(pred[128]{0:T(512)(128)(4,1)} %copy-done.24) | copy-start | bytes 388
  178.0 28.3 %copy-start.19 = (s32[128]{0:T(128)S(1)}, s32[128]{0:T(128)}, u32[]{:S(2)}) copy-start(s32[128]{0:T(128)} %copy-done.18) | copy-start | bytes 1540
  179.0 16.8 %all-to-all-start.6 = ((f32[128,1,512]{2,1,0:T(1,128)}), f32[128,1,512]{2,1,0:T(1,128)}, u32[]{:S(2)}, u32[]{:S(2)}) async-start(f32[128,1,512]{2,1,0:T(1,128)} %copy.30), calls=%async_computation.6 | async-start | bytes 524288 | tf_op jit(solution)/shard_map/all_to_all | solution.py:73
  199.2 16.2 %all-to-all-start.7 = ((f32[128,1,512]{2,1,0:T(1,128)}), f32[128,1,512]{2,1,0:T(1,128)}, u32[]{:S(2)}, u32[]{:S(2)}) async-start(f32[128,1,512]{2,1,0:T(1,128)} %copy.31), calls=%async_computation.7 | async-start | bytes 524288 | tf_op jit(solution)/shard_map/all_to_all | solution.py:68
  204.9 669.8 %reduce-scatter.2.cloned.1.call-start = ((), (), s32[]{:S(2)}) async-start(), calls=%async_computation.10 | async-start | bytes 4227072 | tf_op jit(solution)/shard_map/reduce_scatter | solution.py:135
  215.4 10.7 %copy-start.6 = (f32[512,512]{1,0:T(8,128)S(1)}, f32[512,512]{1,0:T(8,128)}, u32[]{:S(2)}) copy-start(f32[512,512]{1,0:T(8,128)} %convolution_bitcast_fusion.14) | copy-start | bytes 3145732
  215.4 10.7 %copy-start.7 = (f32[512,512]{1,0:T(8,128)S(1)}, f32[512,512]{1,0:T(8,128)}, u32[]{:S(2)}) copy-start(f32[512,512]{1,0:T(8,128)} %convolution_bitcast_fusion.15) | copy-start | bytes 3145732
  215.4 10.7 %copy-start.8 = (f32[512,512]{1,0:T(8,128)S(1)}, f32[512,512]{1,0:T(8,128)}, u32[]{:S(2)}) copy-start(f32[512,512]{1,0:T(8,128)} %convolution_bitcast_fusion.12) | copy-start | bytes 3145732
  215.4 10.7 %copy-start.9 = (f32[512,512]{1,0:T(8,128)S(1)}, f32[512,512]{1,0:T(8,128)}, u32[]{:S(2)}) copy-start(f32[512,512]{1,0:T(8,128)} %convolution_bitcast_fusion.13) | copy-start | bytes 3145732
  215.4 10.7 %copy-start.10 = (f32[512,512]{1,0:T(8,128)S(1)}, f32[512,512]{1,0:T(8,128)}, u32[]{:S(2)}) copy-start(f32[512,512]{1,0:T(8,128)} %convolution_bitcast_fusion.10) | copy-start | bytes 3145732
  215.5 10.7 %copy-start.11 = (f32[512,512]{1,0:T(8,128)S(1)}, f32[512,512]{1,0:T(8,128)}, u32[]{:S(2)}) copy-start(f32[512,512]{1,0:T(8,128)} %convolution_bitcast_fusion.11) | copy-start | bytes 3145732
  232.4 9.4 %copy-start.28 = (f32[512]{0:T(512)S(1)}, f32[512]{0:T(512)}, u32[]{:S(2)}) copy-start(f32[512]{0:T(512)} %get-tuple-element.16) | copy-start | bytes 6148
  232.4 9.4 %copy-start.29 = (f32[512]{0:T(512)S(1)}, f32[512]{0:T(512)}, u32[]{:S(2)}) copy-start(f32[512]{0:T(512)} %get-tuple-element.17) | copy-start | bytes 6148
  232.4 9.4 %copy-start.30 = (f32[512]{0:T(512)S(1)}, f32[512]{0:T(512)}, u32[]{:S(2)}) copy-start(f32[512]{0:T(512)} %get-tuple-element.62) | copy-start | bytes 6148
  232.4 9.4 %copy-start.31 = (f32[512]{0:T(512)S(1)}, f32[512]{0:T(512)}, u32[]{:S(2)}) copy-start(f32[512]{0:T(512)} %get-tuple-element.63) | copy-start | bytes 6148
  232.4 9.4 %copy-start.32 = (f32[512]{0:T(512)S(1)}, f32[512]{0:T(512)}, u32[]{:S(2)}) copy-start(f32[512]{0:T(512)} %get-tuple-element.12) | copy-start | bytes 6148
  232.4 9.4 %copy-start.33 = (f32[512]{0:T(512)S(1)}, f32[512]{0:T(512)}, u32[]{:S(2)}) copy-start(f32[512]{0:T(512)} %get-tuple-element.13) | copy-start | bytes 6148
  232.5 9.4 %copy-start.17 = (s32[128]{0:T(128)S(1)}, s32[128]{0:T(128)}, u32[]{:S(2)}) copy-start(s32[128]{0:T(128)} %copy-done.16) | copy-start | bytes 1540
  233.6 78.0 %copy-start.52 = (pred[128]{0:T(512)(128)(4,1)S(1)}, pred[128]{0:T(512)(128)(4,1)}, u32[]{:S(2)}) copy-start(pred[128]{0:T(512)(128)(4,1)} %get-tuple-element.20) | copy-start | bytes 388
  234.5 77.0 %all-to-all-start.8 = ((f32[128,1,512]{2,1,0:T(1,128)}), f32[128,1,512]{2,1,0:T(1,128)}, u32[]{:S(2)}, u32[]{:S(2)}) async-start(f32[128,1,512]{2,1,0:T(1,128)} %copy.32), calls=%async_computation.8 | async-start | bytes 524288 | tf_op jit(solution)/shard_map/all_to_all | solution.py:73
  243.1 633.0 %copy-start = (f32[128,512]{1,0:T(8,128)}, f32[128,512]{1,0:T(8,128)S(1)}, u32[]{:S(2)}) copy-start(f32[128,512]{1,0:T(8,128)S(1)} %scatter_fusion.3) | copy-start | bytes 786436
  313.2 562.8 %copy-start.1 = (f32[128,512]{1,0:T(8,128)}, f32[128,512]{1,0:T(8,128)S(1)}, u32[]{:S(2)}) copy-start(f32[128,512]{1,0:T(8,128)S(1)} %scatter_custom_fusion.7) | copy-start | bytes 786436
  (17 other events, 107.3 us)
Sparse Core Ops, SparseCore 0:
  232.7 641.9 reduce-scatter.1
where the time goes:
time: 893 us; the launch traced here: 883 us
  waiting for transfers between devices  598 us (67%)
  starting transfers between devices  68.9 us (8%)
  blocking collectives  67.9 us (8%)
  matrix products  66.1 us (7%)
  local copies, waits for them, and re-layouts  48 us (5%)
  other arithmetic  18.8 us (2%)
  between operations  15.2 us (2%)
    reduce_scatter x1, waiting for transfers between devices, per_device(): lax.psum_scatter(weight_total, ('grp', 'own'), scatter_dimension=0, tiled...  561 us
    psum x1, blocking collectives, per_device(): vector_whole = lax.psum(vector_total, ('grp', 'own'))  67.9 us
    all_to_all x4, starting transfers between devices, send_return(): lax.all_to_all(rows_in, ('grp', 'own'), split_axis=0, concat_axis=0, tile...  29.6 us
    all_to_all x4, starting transfers between devices, send_request(): lax.all_to_all(rows_in, ('grp', 'own'), split_axis=0, concat_axis=0, tile...  28.1 us
    all_to_all x4, waiting for transfers between devices, send_return(): lax.all_to_all(rows_in, ('grp', 'own'), split_axis=0, concat_axis=0, tile...  25.2 us
  transfers between devices with their start and end apart: 10, of which 8 were waited for; matrix products, arithmetic and copies ran while one was open for 8% of the time, Pallas kernels for 0%

commit v1 on v0

v1 whole, which is shorter than its diff:
```python
import functools
import math

import jax
import jax.numpy as jnp
from jax import lax
from jax.experimental import pallas as pl
from jax.experimental.pallas import tpu as pltpu
from jax.sharding import PartitionSpec as P

F32 = jnp.float32
BF16 = jnp.bfloat16
MESH = pl.DeviceIdType.MESH

ROWS = 128
D = 512
OWNERS = 128
AUX = 2 * D + 128
WIDE = 384


def device_of(index):
    return (index // 32, index % 32)


def rows_dot(a, b):
    return lax.dot_general(a, b, (((1,), (0,)), ((), ())), preferred_element_type=F32)


def rows_dot_t(a, b):
    return lax.dot_general(a, b, (((1,), (1,)), ((), ())), preferred_element_type=F32)


def permute(onehot, rows):
    high = rows.astype(BF16)
    rest = rows - high.astype(F32)
    middle = rest.astype(BF16)
    low = (rest - middle.astype(F32)).astype(BF16)
    pair = rows_dot(
        jnp.concatenate([onehot, onehot], axis=1), jnp.concatenate([high, middle], axis=0)
    )
    return pair + rows_dot(onehot, low)


def kernel(
    scale,
    user_slot,
    item_slot,
    counts,
    gaps_in,
    user_prev,
    item_prev,
    user_cot,
    item_cot,
    user_weight,
    item_weight,
    bias_time,
    user_out,
    item_out,
    weight_out,
    vector_out,
    v_uslot,
    v_islot,
    v_counts,
    v_gaps,
    v_uprev,
    v_iprev,
    v_ucot,
    v_icot,
    v_uw,
    v_iw,
    v_bias,
    in_sem,
    src,
    dst,
    a2a_send,
    a2a_recv,
    aux_src,
    aux_dst,
    aux_send,
    aux_recv,
    dummy,
    dummy_aux,
    onehots,
    factors,
    prev_t_user,
    prev_t_item,
    low_user_all,
    low_item_all,
    base_user,
    base_item,
    grads_user,
    grads_item,
    live_mine,
    live_here,
    vec,
    vec_core,
    vec_line,
    vec_plane,
    vec_acc,
    weight_acc,
    core_in,
    part_a,
    part_b,
    part_c,
    line_a,
    line_b,
    line_c,
    sum_a,
    sum_b,
    sum_c,
    plane_a,
    plane_b,
    plane_c,
    core_send,
    core_recv,
    line_send,
    line_recv,
    plane_send,
    plane_recv,
):
    grp = lax.axis_index("grp")
    own = lax.axis_index("own")
    me = grp * 32 + own
    my_y = grp
    my_x = own // 8
    my_z = (own // 2) % 4
    my_c = own % 2

    def at(y, x, z, c):
        return (y, x * 8 + z * 2 + c)

    copies = [
        pltpu.make_async_copy(a, b, in_sem.at[i])
        for i, (a, b) in enumerate(
            [
                (item_slot, v_islot),
                (item_cot, v_icot),
                (user_slot, v_uslot),
                (counts, v_counts),
                (gaps_in, v_gaps),
                (user_prev, v_uprev),
                (item_prev, v_iprev),
                (user_weight, v_uw),
                (item_weight, v_iw),
                (bias_time, v_bias),
                (user_cot, v_ucot),
            ]
        )
    ]
    for c in copies:
        c.start()

    barrier = pltpu.get_barrier_semaphore()

    def greet(k, carry):
        pl.semaphore_signal(
            barrier, inc=1, device_id=device_of((me + k) % OWNERS), device_id_type=MESH
        )
        return carry

    lax.fori_loop(1, OWNERS, greet, 0)

    def start_rows(source, target, send_sem, recv_sem):
        def one(k, carry):
            to = (me + k) % OWNERS
            pltpu.make_async_remote_copy(
                src_ref=source.at[pl.ds(to, 1)],
                dst_ref=target.at[pl.ds(me, 1)],
                send_sem=send_sem,
                recv_sem=recv_sem,
                device_id=device_of(to),
                device_id_type=MESH,
            ).start()
            return carry

        lax.fori_loop(1, OWNERS, one, 0)
        target[pl.ds(me, 1)] = source[pl.ds(me, 1)]

    def start_exchange(i):
        start_rows(src.at[i], dst.at[i], a2a_send.at[i], a2a_recv.at[i])

    def wait_bytes(ref, sem):
        pltpu.make_async_copy(ref, ref, sem).wait()

    def arrived(i):
        wait_bytes(dummy.at[pl.ds(0, OWNERS - 1)], a2a_recv.at[i])
        return dst[i]

    def start_aux(i):
        start_rows(aux_src.at[i], aux_dst.at[i], aux_send.at[i], aux_recv.at[i])

    def wait_aux(i):
        wait_bytes(dummy_aux.at[pl.ds(0, OWNERS - 1)], aux_recv.at[i])

    down = lax.broadcasted_iota(jnp.int32, (ROWS, ROWS), 0)
    across = lax.broadcasted_iota(jnp.int32, (ROWS, ROWS), 1)

    def column(row):
        return jnp.sum(jnp.where(down == across, row, 0.0), axis=1, keepdims=True)

    def gather_matrix(slots, b):
        col = column(slots[b].astype(F32))
        return (across.astype(F32) == col).astype(BF16)

    def scatter_matrix(slots, b):
        return (down == slots[b]).astype(BF16)

    def onward_matrix(slots, b):
        return rows_dot(gather_matrix(slots, b), scatter_matrix(slots, b + 1)).astype(BF16)

    copies[0].wait()
    copies[1].wait()
    src[0] = permute(gather_matrix(v_islot, 3), v_icot[...])
    pl.semaphore_wait(barrier, OWNERS - 1)
    start_exchange(0)

    for i in range(3, 7):
        copies[i].wait()

    def fill_aux(i, b):
        aux_src[i, :, 0:D] = v_uprev[b].astype(F32)
        aux_src[i, :, D : 2 * D] = v_iprev[b].astype(F32)
        gap = column(v_gaps[pl.ds(b, 1)])
        live = column((v_counts[b] > 0).astype(F32))
        lane = lax.broadcasted_iota(jnp.int32, (ROWS, 128), 1)
        aux_src[i, :, 2 * D :] = jnp.where(lane == 0, gap, jnp.where(lane == 1, live, 0.0))

    fill_aux(0, 2)
    start_aux(0)

    for i in range(7, 11):
        copies[i].wait()
    copies[2].wait()

    def user_factor(u, i, gap, live):
        pre = (
            rows_dot(u, v_uw[0:D])
            + rows_dot(i, v_uw[D : 2 * D])
            + gap * v_bias[1:2]
            + v_bias[0:1]
        )
        state = jnp.tanh(pre)
        return live * (1.0 - state * state)

    def item_factor(u, i, gap, live):
        pre = (
            rows_dot(i, v_iw[0:D])
            + rows_dot(u, v_iw[D : 2 * D])
            + gap * v_bias[3:4]
            + v_bias[2:3]
        )
        state = jnp.tanh(pre)
        return live * (1.0 - state * state)

    def mine(b):
        gap = column(v_gaps[pl.ds(b, 1)])
        live = column((v_counts[b] > 0).astype(F32))
        return v_uprev[b], v_iprev[b], gap, live

    def here(i):
        u = aux_dst[i, :, 0:D].astype(BF16)
        it = aux_dst[i, :, D : 2 * D].astype(BF16)
        return u, it, aux_dst[i, :, 2 * D : 2 * D + 1], aux_dst[i, :, 2 * D + 1 : 2 * D + 2]

    def keep_transposed(ref, b, u, i, user_first):
        cols = slice(b * ROWS, (b + 1) * ROWS)
        first, second = (u, i) if user_first else (i, u)
        ref[0:D, cols] = first.T
        ref[D : 2 * D, cols] = second.T

    def add_vectors(row, delta, gap):
        vec[row : row + 1] += jnp.sum(delta, axis=0, keepdims=True)
        vec[row + 1 : row + 2] += jnp.sum(gap * delta, axis=0, keepdims=True)

    vec[...] = jnp.zeros_like(vec)

    def keep_low(ref, b, low):
        ref[b * ROWS : (b + 1) * ROWS] = low

    u3, i3, gap3, live3 = mine(3)
    factors[0] = item_factor(u3, i3, gap3, live3)
    grad_user = permute(gather_matrix(v_uslot, 3), v_ucot[...])
    grads_user[...] = grad_user
    delta_user = user_factor(u3, i3, gap3, live3) * grad_user
    low_user = delta_user.astype(BF16)
    keep_low(low_user_all, 3, low_user)
    base_item[...] = rows_dot_t(low_user, v_uw[D : 2 * D])
    base_user[...] = rows_dot_t(low_user, v_uw[0:D])
    add_vectors(0, delta_user, gap3)
    keep_transposed(prev_t_user, 3, u3, i3, True)
    keep_transposed(prev_t_item, 3, u3, i3, False)
    onehots[0] = onward_matrix(v_uslot, 2)
    onehots[1] = onward_matrix(v_islot, 2)
    fill_aux(1, 0)

    grad_item = arrived(0)
    delta_item = factors[0] * grad_item
    low_item = delta_item.astype(BF16)
    new_item = base_item[...] + rows_dot_t(low_item, v_iw[0:D])
    src[1] = jnp.where(live3 > 0.0, new_item, grad_item)
    start_exchange(1)
    new_user = base_user[...] + rows_dot_t(low_item, v_iw[D : 2 * D])
    src[2] = permute(onehots[0], jnp.where(live3 > 0.0, new_user, grads_user[...]))
    start_exchange(2)
    keep_low(low_item_all, 3, low_item)
    add_vectors(2, factors[0] * dst[0], gap3)
    start_aux(1)

    wait_aux(0)
    u2, i2, gap2, live2 = here(0)
    factors[0] = user_factor(u2, i2, gap2, live2)
    factors[1] = item_factor(u2, i2, gap2, live2)
    keep_transposed(prev_t_user, 2, u2, i2, True)
    keep_transposed(prev_t_item, 2, u2, i2, False)
    onehots[2] = onward_matrix(v_uslot, 1)
    onehots[3] = onward_matrix(v_islot, 1)

    grad_item = permute(onehots[1], arrived(1))
    delta_item = factors[1] * grad_item
    low_item = delta_item.astype(BF16)
    grad_user = arrived(2)
    delta_user = factors[0] * grad_user
    low_user = delta_user.astype(BF16)
    new_user = rows_dot_t(low_user, v_uw[0:D]) + rows_dot_t(low_item, v_iw[D : 2 * D])
    src[3] = jnp.where(live2 > 0.0, new_user, grad_user)
    start_exchange(3)
    new_item = rows_dot_t(low_user, v_uw[D : 2 * D]) + rows_dot_t(low_item, v_iw[0:D])
    src[4] = permute(onehots[3], jnp.where(live2 > 0.0, new_item, grad_item))
    start_exchange(4)
    keep_low(low_user_all, 2, low_user)
    keep_low(low_item_all, 2, low_item)
    add_vectors(0, delta_user, gap2)
    add_vectors(2, delta_item, gap2)

    u1, i1, gap1, live1 = mine(1)
    factors[0] = user_factor(u1, i1, gap1, live1)
    factors[1] = item_factor(u1, i1, gap1, live1)
    keep_transposed(prev_t_user, 1, u1, i1, True)
    keep_transposed(prev_t_item, 1, u1, i1, False)
    u0, i0, gap0, live0 = mine(0)
    factors[2] = user_factor(u0, i0, gap0, live0)
    keep_transposed(prev_t_user, 0, u0, i0, True)
    onehots[4] = onward_matrix(v_uslot, 0)
    onehots[5] = onward_matrix(v_islot, 0)

    grad_user = permute(onehots[2], arrived(3))
    delta_user = factors[0] * grad_user
    low_user = delta_user.astype(BF16)
    grad_item = arrived(4)
    delta_item = factors[1] * grad_item
    low_item = delta_item.astype(BF16)
    new_item = rows_dot_t(low_user, v_uw[D : 2 * D]) + rows_dot_t(low_item, v_iw[0:D])
    src[5] = jnp.where(live1 > 0.0, new_item, grad_item)
    start_exchange(5)
    new_user = rows_dot_t(low_user, v_uw[0:D]) + rows_dot_t(low_item, v_iw[D : 2 * D])
    grad_user0 = permute(onehots[4], jnp.where(live1 > 0.0, new_user, grad_user))
    grads_user[...] = grad_user0
    delta_user0 = factors[2] * grad_user0
    low_user0 = delta_user0.astype(BF16)
    src[6] = low_user0.astype(F32)
    start_exchange(6)
    keep_low(low_user_all, 1, low_user)
    keep_low(low_item_all, 1, low_item)
    keep_low(low_user_all, 0, low_user0)
    add_vectors(0, delta_user, gap1)
    add_vectors(2, delta_item, gap1)
    add_vectors(0, delta_user0, gap0)

    sibling = at(my_y, my_x, my_z, 1 - my_c)

    def core_copy(half):
        blocks = pl.ds(half * 32, 32)
        return pltpu.make_async_remote_copy(
            src_ref=weight_acc.at[blocks, 1 - my_c],
            dst_ref=core_in.at[blocks],
            send_sem=core_send.at[half],
            recv_sem=core_recv.at[half],
            device_id=sibling,
            device_id_type=MESH,
        )

    for q in range(4):
        rows = slice(q * 256, (q + 1) * 256)
        weight_acc[q * 8 : (q + 1) * 8] = rows_dot(prev_t_user[rows], low_user_all[...]).reshape(
            8, 2, 16, D
        )
    core_copy(0).start()
    for q in range(4):
        rows = slice(q * 256, (q + 1) * 256)
        weight_acc[32 + q * 8 : 32 + (q + 1) * 8] = rows_dot(
            prev_t_item[rows, ROWS:], low_item_all[ROWS:]
        ).reshape(8, 2, 16, D)

    def add_core(half):
        def one(n, carry):
            y = n // 16
            x = (n // 4) % 4
            z = n % 4
            total = weight_acc[n, my_c] + core_in[n]
            part_a[x, y * 4 + z] = total[0:8, 0:WIDE]
            part_b[y, x * 4 + z] = total[8:16, 0:WIDE]
            part_c[z, y * 4 + x] = total[:, WIDE:]
            return carry

        lax.fori_loop(half * 32, half * 32 + 32, one, 0)

    wait_aux(1)
    u0h, i0h, gap0h, live0h = here(1)
    factors[0] = item_factor(u0h, i0h, gap0h, live0h)
    keep_transposed(prev_t_item, 0, u0h, i0h, False)
    core_copy(0).wait()
    add_core(0)

    grad_item = permute(onehots[5], arrived(5))
    delta_item = factors[0] * grad_item
    low_item0 = delta_item.astype(BF16)
    for q in range(4):
        rows = slice(q * 256, (q + 1) * 256)
        blocks = slice(32 + q * 8, 32 + (q + 1) * 8)
        weight_acc[blocks] += rows_dot(prev_t_item[rows, 0:ROWS], low_item0).reshape(8, 2, 16, D)
    core_copy(1).start()
    add_vectors(2, delta_item, gap0h)
    vec_to_core = pltpu.make_async_remote_copy(
        src_ref=vec,
        dst_ref=vec_core,
        send_sem=core_send.at[2],
        recv_sem=core_recv.at[2],
        device_id=sibling,
        device_id_type=MESH,
    )
    vec_to_core.start()
    src[7] = low_item0.astype(F32)
    start_exchange(7)
    grads_item[...] = grad_item
    core_copy(1).wait()
    add_core(1)
    vec_to_core.wait()
    vec_acc[0] = vec[...] + vec_core[...]

    def line_copies(d):
        x, y, z = (my_x + d) % 4, (my_y + d) % 4, (my_z + d) % 4
        specs = [
            (part_a.at[x], line_a.at[d - 1], at(my_y, x, my_z, my_c)),
            (part_b.at[y], line_b.at[d - 1], at(y, my_x, my_z, my_c)),
            (part_c.at[z], line_c.at[d - 1], at(my_y, my_x, z, my_c)),
            (vec_acc.at[0], vec_line.at[d - 1], at(my_y, x, my_z, my_c)),
        ]
        return [
            pltpu.make_async_remote_copy(
                src_ref=s,
                dst_ref=t,
                send_sem=line_send.at[d - 1, i],
                recv_sem=line_recv.at[d - 1, i],
                device_id=device,
                device_id_type=MESH,
            )
            for i, (s, t, device) in enumerate(specs)
        ]

    lines = [line_copies(d) for d in (2, 1, 3)]
    for group in lines:
        for c in group:
            c.start()

    low_user0h = arrived(6).astype(BF16)
    new_item = rows_dot_t(low_user0h, v_uw[D : 2 * D]) + rows_dot_t(low_item0, v_iw[0:D])
    item_out[...] = permute(
        scatter_matrix(v_islot, 0), jnp.where(live0h > 0.0, new_item, grads_item[...])
    )

    for group in lines:
        for c in group:
            c.wait_recv()
    sum_a[...] = part_a[my_x] + line_a[0] + line_a[1] + line_a[2]
    sum_b[...] = part_b[my_y] + line_b[0] + line_b[1] + line_b[2]
    sum_c[...] = part_c[my_z] + line_c[0] + line_c[1] + line_c[2]
    vec_acc[1] = vec_acc[0] + vec_line[0] + vec_line[1] + vec_line[2]

    def plane_specs(n):
        d, e = n // 4, n % 4
        ay, az = (my_y + d) % 4, (my_z + e) % 4
        bx, bz = (my_x + d) % 4, (my_z + e) % 4
        cy, cx = (my_y + d) % 4, (my_x + e) % 4
        specs = [
            (sum_a.at[ay * 4 + az], plane_a.at[n - 1], at(ay, my_x, az, my_c)),
            (sum_b.at[bx * 4 + bz], plane_b.at[n - 1], at(my_y, bx, bz, my_c)),
            (sum_c.at[cy * 4 + cx], plane_c.at[n - 1], at(cy, cx, my_z, my_c)),
            (vec_acc.at[1], vec_plane.at[n - 1], at(ay, my_x, az, my_c)),
        ]
        return [
            pltpu.make_async_remote_copy(
                src_ref=s,
                dst_ref=t,
                send_sem=plane_send.at[i],
                recv_sem=plane_recv.at[i],
                device_id=device,
                device_id_type=MESH,
            )
            for i, (s, t, device) in enumerate(specs)
        ]

    def start_plane(n, carry):
        for c in plane_specs(n):
            c.start()
        return carry

    lax.fori_loop(1, 16, start_plane, 0)

    low_item0s = arrived(7).astype(BF16)
    low_user0 = low_user_all[0:ROWS]
    new_user = rows_dot_t(low_user0, v_uw[0:D]) + rows_dot_t(low_item0s, v_iw[D : 2 * D])
    live0 = column((v_counts[0] > 0).astype(F32))
    user_out[...] = permute(
        scatter_matrix(v_uslot, 0), jnp.where(live0 > 0.0, new_user, grads_user[...])
    )

    planes = [plane_a, plane_b, plane_c, vec_plane]
    for i, ref in enumerate(planes):
        wait_bytes(ref, plane_recv.at[i])

    def total(own_part, ref):
        result = own_part
        for n in range(15):
            result = result + ref[n]
        return result * scale

    weight_out[0:8, 0:WIDE] = total(sum_a[my_y * 4 + my_z], plane_a)
    weight_out[8:16, 0:WIDE] = total(sum_b[my_x * 4 + my_z], plane_b)
    weight_out[:, WIDE:] = total(sum_c[my_y * 4 + my_x], plane_c)
    vector_out[...] = total(vec_acc[1], vec_plane)[0:4]

    for i in range(8):
        wait_bytes(dummy.at[pl.ds(0, OWNERS - 1)], a2a_send.at[i])
    for i in range(2):
        wait_bytes(dummy_aux.at[pl.ds(0, OWNERS - 1)], aux_send.at[i])
    for group in lines:
        for c in group:
            c.wait_send()
    for i, ref in enumerate(planes):
        wait_bytes(ref, plane_send.at[i])


def per_device(*arrays):
    user_prev = arrays[4]
    batches = user_prev.shape[0]
    scale = 1.0 / math.sqrt(batches * OWNERS * ROWS)
    any_spec = pl.BlockSpec(memory_space=pl.ANY)
    vmem_spec = pl.BlockSpec(memory_space=pltpu.VMEM)
    vmem = pltpu.VMEM
    dma = pltpu.SemaphoreType.DMA
    scratch = [vmem(a.shape, a.dtype) for a in arrays]
    scratch += [
        dma((11,)),
        vmem((8, ROWS, D), F32),
        vmem((8, ROWS, D), F32),
        dma((8,)),
        dma((8,)),
        vmem((2, ROWS, AUX), F32),
        vmem((2, ROWS, AUX), F32),
        dma((2,)),
        dma((2,)),
        vmem((ROWS, 1, D), F32),
        vmem((ROWS, 1, AUX), F32),
        vmem((6, ROWS, ROWS), BF16),
        vmem((3, ROWS, D), F32),
        vmem((2 * D, 4 * ROWS), BF16),
        vmem((2 * D, 4 * ROWS), BF16),
        vmem((4 * ROWS, D), BF16),
        vmem((4 * ROWS, D), BF16),
        vmem((ROWS, D), F32),
        vmem((ROWS, D), F32),
        vmem((ROWS, D), F32),
        vmem((ROWS, D), F32),
        vmem((ROWS, 128), F32),
        vmem((ROWS, 128), F32),
        vmem((8, D), F32),
        vmem((8, D), F32),
        vmem((3, 8, D), F32),
        vmem((15, 8, D), F32),
        vmem((2, 8, D), F32),
        vmem((64, 2, 16, D), F32),
        vmem((64, 16, D), F32),
        vmem((4, 16, 8, WIDE), F32),
        vmem((4, 16, 8, WIDE), F32),
        vmem((4, 16, 16, D - WIDE), F32),
        vmem((3, 16, 8, WIDE), F32),
        vmem((3, 16, 8, WIDE), F32),
        vmem((3, 16, 16, D - WIDE), F32),
        vmem((16, 8, WIDE), F32),
        vmem((16, 8, WIDE), F32),
        vmem((16, 16, D - WIDE), F32),
        vmem((15, 8, WIDE), F32),
        vmem((15, 8, WIDE), F32),
        vmem((15, 16, D - WIDE), F32),
        dma((3,)),
        dma((3,)),
        dma((3, 4)),
        dma((3, 4)),
        dma((4,)),
        dma((4,)),
    ]
    return pl.pallas_call(
        functools.partial(kernel, scale),
        out_shape=(
            jax.ShapeDtypeStruct((ROWS, D), F32),
            jax.ShapeDtypeStruct((ROWS, D), F32),
            jax.ShapeDtypeStruct((16, D), F32),
            jax.ShapeDtypeStruct((4, D), F32),
        ),
        in_specs=[any_spec] * 11,
        out_specs=(vmem_spec,) * 4,
        scratch_shapes=scratch,
        compiler_params=pltpu.CompilerParams(
            collective_id=0, has_side_effects=True, vmem_limit_bytes=56 * 2**20
        ),
        cost_estimate=pl.CostEstimate(
            flops=12_000_000_000, bytes_accessed=5_000_000, transcendentals=600_000
        ),
    )(*arrays)


def solution(mesh):
    both = ("grp", "own")
    in_specs = (
        P(None, both, None),
        P(None, both, None),
        P(None, both, None),
        P(None, both),
        P(None, both, None),
        P(None, both, None),
        P(both, None),
        P(both, None),
        P(),
        P(),
        P(),
    )
    out_specs = (P(both, None), P(both, None), P(both, None), P())
    return jax.shard_map(
        per_device, mesh=mesh, in_specs=in_specs, out_specs=out_specs, check_vma=False
    )
```

time: 893 us -> 88.7 us (0.10); the launches traced: 883 us -> 88.5 us
  waiting for transfers between devices: 598 us -> 0 us
  Pallas kernels: 0 us -> 84.1 us
  starting transfers between devices: 68.9 us -> 0 us
  blocking collectives: 67.9 us -> 0 us
  matrix products: 66.1 us -> 0 us
  local copies, waits for them, and re-layouts: 48 us -> 3.78 us
  other arithmetic: 18.8 us -> 0 us
  between operations: 15.2 us -> 0.66 us
    reduce_scatter x1 -> x0, waiting for transfers between devices: 561 us -> none  [per_device(): lax.psum_scatter(weight_total, ('grp', 'own'), scatter_dimension=0, tiled...]
    pallas_call x0 -> x1, Pallas kernels: none -> 84.1 us  [per_device(): pl.pallas_call(functools.partial(kernel, scale), out_shape=(jax.ShapeDtyp...]
    all_to_all x9 -> x0, starting transfers between devices: 68.8 us -> none  [the longest x4 29.6 us: send_return(): lax.all_to_all(rows_in, ('grp', 'own'), split_axis=0, concat_axis=0, tile...]
    psum x1 -> x0, blocking collectives: 67.9 us -> none  [per_device(): vector_whole = lax.psum(vector_total, ('grp', 'own'))]
    dot_general x48 -> x0, matrix products: 66.1 us -> none  [the longest x4 9.05 us: backward_rows(): jnp.dot(item_rows.T, low_user, preferred_element_type=jnp.float32)]
    all_to_all x9 -> x0, waiting for transfers between devices: 36.7 us -> none  [the longest x4 25.2 us: send_return(): lax.all_to_all(rows_in, ('grp', 'own'), split_axis=0, concat_axis=0, tile...]
    slice x3 -> x0, local copies, waits for them, and re-layouts: 20.4 us -> none  [the longest x1 10.2 us: per_device(): live_got[position][:, None]]
    gather x8 -> x0, local copies, waits for them, and re-layouts: 9.08 us -> none  [the longest x4 5.93 us: per_device(): grad_user = adj_users[slot_users[position]]]
  transfers between devices with their start and end apart: 10 -> 0, of which waited for: 8 -> 0; matrix products, arithmetic and copies ran while one was open for 8% -> 0% of each run, Pallas kernels for 0% -> 0%
where the time goes in v1:
time: 88.7 us; the launch traced here: 88.5 us
  Pallas kernels  84.1 us (95%)
  local copies, waits for them, and re-layouts  3.78 us (4%)
    pallas_call x1, Pallas kernels, per_device(): pl.pallas_call(functools.partial(kernel, scale), out_shape=(jax.ShapeDtyp...  84.1 us
    unnamed x10, local copies, waits for them, and re-layouts  3.78 us

profile of v1, /device:TPU:0, one launch (start us, length us, event | category | flops | bytes accessed | tf_op | source)
XLA Modules:
  0.0 88.5 jit_solution(18407246363907953602)
XLA Ops:
  0.6 84.1 %shard_map.138 = (f32[128,512]{1,0:T(8,128)}, f32[128,512]{1,0:T(8,128)}, f32[16,512]{1,0:T(8,128)}, f32[4,512]{1,0:T(4,128)}) custom-call(s32[4,1,128]{2,1,0:T(1,128)} %user_slot.1, s32[4,1,128]{2,1,0:T(1,128)} %item_slot.1, s32[4,1,128]{2,1,0:T(1,128)} %counts.1, f32[4,128]{1,0:T(4,128)} %gaps_in.1, bf16[4,128,512]{2,1,0:T(8,128)(2,1)} %user_prev.1, ...), custom_call_target="tpu_custom_call" | custom-call | flops 12000000000 | bytes 5000000 | tf_op jit(solution)/shard_map/pallas_call | solution.py:603
  84.7 0.0 copy-start
  84.7 1.7 %copy.19 = f32[128,512]{1,0:T(8,128)} copy(f32[128,512]{1,0:T(8,128)} %get-tuple-element.8) | data formatting | bytes 524288
  86.4 0.0 copy-done
  86.4 0.0 copy-start.1
  86.4 0.7 copy.20
  87.1 0.1 copy-done.1
  87.2 0.0 copy-start.2
  87.2 0.6 copy.21
  87.8 0.1 copy-done.2
  87.9 0.6 copy.22
Async XLA Ops:
  84.7 1.7 %copy-start = (f32[128,512]{1,0:T(8,128)S(1)}, f32[128,512]{1,0:T(8,128)}, u32[]{:S(2)}) copy-start(f32[128,512]{1,0:T(8,128)} %get-tuple-element.9) | copy-start | bytes 786436
  86.4 0.8 copy-start.1
  87.2 0.7 copy-start.2

commit v2 on v1

v2 whole, which is shorter than its diff:
```python
import functools
import math

import jax
import jax.numpy as jnp
from jax import lax
from jax.experimental import pallas as pl
from jax.experimental.pallas import tpu as pltpu
from jax.sharding import PartitionSpec as P

F32 = jnp.float32
BF16 = jnp.bfloat16
MESH = pl.DeviceIdType.MESH

ROWS = 128
D = 512
OWNERS = 128
AUX = D + 128
WIDE = 384


def device_of(index):
    return (index // 32, index % 32)


def rows_dot(a, b):
    return lax.dot_general(a, b, (((1,), (0,)), ((), ())), preferred_element_type=F32)


def rows_dot_t(a, b):
    return lax.dot_general(a, b, (((1,), (1,)), ((), ())), preferred_element_type=F32)


def permute(onehot, rows):
    high = rows.astype(BF16)
    rest = rows - high.astype(F32)
    middle = rest.astype(BF16)
    low = (rest - middle.astype(F32)).astype(BF16)
    pair = rows_dot(
        jnp.concatenate([onehot, onehot], axis=1), jnp.concatenate([high, middle], axis=0)
    )
    return pair + rows_dot(onehot, low)


def kernel(
    scale,
    user_slot,
    item_slot,
    counts,
    gaps_in,
    user_prev,
    item_prev,
    user_cot,
    item_cot,
    user_weight,
    item_weight,
    bias_time,
    user_out,
    item_out,
    weight_out,
    vector_out,
    v_uslot,
    v_islot,
    v_counts,
    v_gaps,
    v_uprev,
    v_iprev,
    v_ucot,
    v_icot,
    v_uw,
    v_iw,
    v_bias,
    in_sem,
    src,
    dst,
    a2a_send,
    a2a_recv,
    aux_src,
    aux_dst,
    aux_send,
    aux_recv,
    dummy,
    dummy_aux,
    onehots,
    factors,
    prev_t,
    prev_t_here,
    low_user_all,
    low_item_all,
    base_user,
    base_item,
    grads_user,
    grads_item,
    vec,
    vec_core,
    vec_line,
    vec_plane,
    vec_acc,
    weight_acc,
    core_in,
    part_a,
    part_b,
    part_c,
    line_a,
    line_b,
    line_c,
    sum_a,
    sum_b,
    sum_c,
    plane_a,
    plane_b,
    plane_c,
    core_send,
    core_recv,
    line_send,
    line_recv,
    plane_send,
    plane_recv,
    v_item_out,
    v_user_out,
    out_sem,
):
    grp = lax.axis_index("grp")
    own = lax.axis_index("own")
    me = grp * 32 + own
    my_y = grp
    my_x = own // 8
    my_z = (own // 2) % 4
    my_c = own % 2

    def at(y, x, z, c):
        return (y, x * 8 + z * 2 + c)

    loads = {
        name: pltpu.make_async_copy(a, b, in_sem.at[i])
        for i, (name, a, b) in enumerate(
            [
                ("islot", item_slot, v_islot),
                ("icot", item_cot, v_icot),
                ("counts", counts, v_counts),
                ("gaps", gaps_in, v_gaps),
                ("bias", bias_time, v_bias),
                ("iprev", item_prev, v_iprev),
                ("uprev", user_prev, v_uprev),
                ("iw", item_weight, v_iw),
                ("uw", user_weight, v_uw),
                ("uslot", user_slot, v_uslot),
                ("ucot", user_cot, v_ucot),
            ]
        )
    }
    for load in loads.values():
        load.start()

    barrier = pltpu.get_barrier_semaphore()

    def greet(k, carry):
        pl.semaphore_signal(
            barrier, inc=1, device_id=device_of((me + k) % OWNERS), device_id_type=MESH
        )
        return carry

    lax.fori_loop(1, OWNERS, greet, 0)

    def start_rows(source, target, send_sem, recv_sem):
        def one(k, carry):
            to = (me + k) % OWNERS
            pltpu.make_async_remote_copy(
                src_ref=source.at[pl.ds(to, 1)],
                dst_ref=target.at[pl.ds(me, 1)],
                send_sem=send_sem,
                recv_sem=recv_sem,
                device_id=device_of(to),
                device_id_type=MESH,
            ).start()
            return carry

        lax.fori_loop(1, OWNERS, one, 0)
        target[pl.ds(me, 1)] = source[pl.ds(me, 1)]

    def wait_bytes(ref, sem):
        pltpu.make_async_copy(ref, ref, sem).wait()

    def start_exchange(i):
        start_rows(src.at[i], dst.at[i], a2a_send.at[i], a2a_recv.at[i])

    def arrived(i):
        wait_bytes(dummy.at[pl.ds(0, OWNERS - 1)], a2a_recv.at[i])
        return dst[i]

    def sent(i):
        wait_bytes(dummy.at[pl.ds(0, OWNERS - 1)], a2a_send.at[i])

    def start_aux():
        start_rows(aux_src, aux_dst, aux_send, aux_recv)

    def wait_aux():
        wait_bytes(dummy_aux.at[pl.ds(0, OWNERS - 1)], aux_recv)

    def sent_aux():
        wait_bytes(dummy_aux.at[pl.ds(0, OWNERS - 1)], aux_send)

    down = lax.broadcasted_iota(jnp.int32, (ROWS, ROWS), 0)
    across = lax.broadcasted_iota(jnp.int32, (ROWS, ROWS), 1)

    def column(row):
        return jnp.sum(jnp.where(down == across, row, 0.0), axis=1, keepdims=True)

    def gather_matrix(slots, b):
        col = column(slots[b].astype(F32))
        return (across.astype(F32) == col).astype(BF16)

    def scatter_matrix(slots, b):
        return (down == slots[b]).astype(BF16)

    def onward_matrix(slots, b):
        return rows_dot(gather_matrix(slots, b), scatter_matrix(slots, b + 1)).astype(BF16)

    loads["islot"].wait()
    loads["icot"].wait()
    src[0] = permute(gather_matrix(v_islot, 3), v_icot[...])
    pl.semaphore_wait(barrier, OWNERS - 1)
    start_exchange(0)

    for name in ("counts", "gaps", "bias", "iprev", "uprev", "iw", "uw", "uslot", "ucot"):
        loads[name].wait()

    def user_factor(u, i, gap):
        pre = (
            rows_dot(u, v_uw[0:D])
            + rows_dot(i, v_uw[D : 2 * D])
            + gap * v_bias[1:2]
            + v_bias[0:1]
        )
        state = jnp.tanh(pre)
        return 1.0 - state * state

    def item_factor(u, i, gap):
        pre = (
            rows_dot(i, v_iw[0:D])
            + rows_dot(u, v_iw[D : 2 * D])
            + gap * v_bias[3:4]
            + v_bias[2:3]
        )
        state = jnp.tanh(pre)
        return 1.0 - state * state

    def saved(b):
        gap = column(v_gaps[pl.ds(b, 1)])
        live = column((v_counts[b] > 0).astype(F32))
        return v_uprev[b], v_iprev[b], gap, live

    def keep_transposed(b, u, i):
        prev_t[0:D, b * ROWS : (b + 1) * ROWS] = u.T
        prev_t[D : 2 * D, b * ROWS : (b + 1) * ROWS] = i.T

    def keep_low(ref, b, low):
        ref[b * ROWS : (b + 1) * ROWS] = low

    def add_vectors(row, delta, gap):
        vec[row : row + 1] += jnp.sum(delta, axis=0, keepdims=True)
        vec[row + 1 : row + 2] += jnp.sum(gap * delta, axis=0, keepdims=True)

    vec[...] = jnp.zeros_like(vec)

    u2, i2, gap2, live2 = saved(2)
    src[8] = jnp.where(live2 > 0.0, item_factor(u2, i2, gap2), -1.0)
    start_exchange(8)

    u3, i3, gap3, live3 = saved(3)
    factors[0] = live3 * item_factor(u3, i3, gap3)
    grad_user = permute(gather_matrix(v_uslot, 3), v_ucot[...])
    grads_user[...] = grad_user
    delta_user = live3 * user_factor(u3, i3, gap3) * grad_user
    low_user = delta_user.astype(BF16)
    keep_low(low_user_all, 3, low_user)
    base_item[...] = rows_dot_t(low_user, v_uw[D : 2 * D])
    base_user[...] = rows_dot_t(low_user, v_uw[0:D])
    add_vectors(0, delta_user, gap3)
    factors[1] = live2 * user_factor(u2, i2, gap2)
    onehots[0] = onward_matrix(v_uslot, 2)
    onehots[1] = onward_matrix(v_islot, 2)

    grad_item = arrived(0)
    low_item = (factors[0] * grad_item).astype(BF16)
    new_item = base_item[...] + rows_dot_t(low_item, v_iw[0:D])
    src[1] = jnp.where(live3 > 0.0, new_item, grad_item)
    start_exchange(1)
    new_user = base_user[...] + rows_dot_t(low_item, v_iw[D : 2 * D])
    grad_user = permute(onehots[0], jnp.where(live3 > 0.0, new_user, grads_user[...]))
    delta_user = factors[1] * grad_user
    low_user = delta_user.astype(BF16)
    src[2] = low_user.astype(F32)
    start_exchange(2)
    grads_user[...] = grad_user
    keep_low(low_item_all, 3, low_item)
    keep_low(low_user_all, 2, low_user)
    add_vectors(2, factors[0] * dst[0], gap3)
    add_vectors(0, delta_user, gap2)
    base_user[...] = rows_dot_t(low_user, v_uw[0:D])

    onehots[2] = onward_matrix(v_uslot, 1)
    onehots[3] = onward_matrix(v_islot, 1)
    u1, i1, gap1, live1 = saved(1)
    factors[0] = live1 * user_factor(u1, i1, gap1)
    factors[1] = live1 * item_factor(u1, i1, gap1)
    keep_transposed(3, u3, i3)
    keep_transposed(2, u2, i2)

    src[9] = v_uprev[0].astype(F32)
    start_exchange(9)

    factor = arrived(8)
    grad_item = permute(onehots[1], arrived(1))
    delta_item = jnp.where(factor > -0.5, factor * grad_item, 0.0)
    src[3] = delta_item
    start_exchange(3)
    low_item = delta_item.astype(BF16)
    part = rows_dot_t(low_item, v_iw[0:D])
    low_user = arrived(2).astype(BF16)
    new_item = rows_dot_t(low_user, v_uw[D : 2 * D]) + part
    src[4] = permute(onehots[3], jnp.where(factor > -0.5, new_item, grad_item))
    start_exchange(4)

    u0, i0, gap0, live0 = saved(0)
    lane = lax.broadcasted_iota(jnp.int32, (ROWS, 128), 1)
    aux_src[:, 0:D] = i0.astype(F32)
    aux_src[:, D:] = jnp.where(lane == 0, gap0, jnp.where(lane == 1, live0, 0.0))
    factors[2] = live0 * user_factor(u0, i0, gap0)
    keep_transposed(1, u1, i1)
    keep_transposed(0, u0, i0)
    onehots[4] = onward_matrix(v_uslot, 0)
    onehots[5] = onward_matrix(v_islot, 0)
    start_aux()

    delta_item = arrived(3)
    low_item = delta_item.astype(BF16)
    new_user = base_user[...] + rows_dot_t(low_item, v_iw[D : 2 * D])
    keep_low(low_item_all, 2, low_item)
    grad_user = permute(onehots[2], jnp.where(live2 > 0.0, new_user, grads_user[...]))
    delta_user = factors[0] * grad_user
    low_user = delta_user.astype(BF16)
    keep_low(low_user_all, 1, low_user)
    base_item[...] = rows_dot_t(low_user, v_uw[D : 2 * D])
    base_user[...] = rows_dot_t(low_user, v_uw[0:D])
    grads_user[...] = grad_user
    add_vectors(2, delta_item, gap2)
    add_vectors(0, delta_user, gap1)

    grad_item = arrived(4)
    low_item = (factors[1] * grad_item).astype(BF16)
    new_item = base_item[...] + rows_dot_t(low_item, v_iw[0:D])
    src[5] = jnp.where(live1 > 0.0, new_item, grad_item)
    start_exchange(5)
    new_user = base_user[...] + rows_dot_t(low_item, v_iw[D : 2 * D])
    grad_user = permute(onehots[4], jnp.where(live1 > 0.0, new_user, grads_user[...]))
    delta_user = factors[2] * grad_user
    low_user = delta_user.astype(BF16)
    src[6] = low_user.astype(F32)
    keep_low(low_item_all, 1, low_item)
    keep_low(low_user_all, 0, low_user)
    grads_user[...] = grad_user

    sibling = at(my_y, my_x, my_z, 1 - my_c)

    def core_copy(y):
        blocks = pl.ds(y * 16, 16)
        return pltpu.make_async_remote_copy(
            src_ref=weight_acc.at[blocks, 1 - my_c],
            dst_ref=core_in.at[blocks],
            send_sem=core_send.at[y],
            recv_sem=core_recv.at[y],
            device_id=sibling,
            device_id_type=MESH,
        )

    for q in range(4):
        rows = slice(q * 256, (q + 1) * 256)
        weight_acc[q * 8 : (q + 1) * 8] = rows_dot(prev_t[rows], low_user_all[...]).reshape(
            8, 2, 16, D
        )
    core_copy(0).start()
    core_copy(1).start()
    add_vectors(2, factors[1] * dst[4], gap1)
    add_vectors(0, delta_user, gap0)
    base_user[...] = rows_dot_t(low_user, v_uw[0:D])

    for q in range(4):
        rows = slice(((q + 2) % 4) * 256, ((q + 2) % 4 + 1) * 256)
        weight_acc[32 + q * 8 : 32 + (q + 1) * 8] = rows_dot(
            prev_t[rows, ROWS:], low_item_all[ROWS:]
        ).reshape(8, 2, 16, D)

    start_exchange(6)

    wait_bytes(dummy.at[pl.ds(0, OWNERS - 1)], a2a_recv.at[9])
    wait_aux()
    u0h = dst[9].astype(BF16)
    i0h = aux_dst[:, 0:D].astype(BF16)
    gap0h = aux_dst[:, D : D + 1]
    live0h = aux_dst[:, D + 1 : D + 2]
    factors[0] = live0h * item_factor(u0h, i0h, gap0h)
    prev_t_here[0:D] = i0h.T
    prev_t_here[D : 2 * D] = u0h.T

    def add_core(to_y):
        def one(n, carry):
            x = n // 4
            z = n % 4
            block = to_y * 16 + n
            total = weight_acc[block, my_c] + core_in[block]
            part_a[x, to_y * 4 + z] = total[0:8, 0:WIDE]
            part_b[z, to_y * 4 + x] = total[8:16, 0:WIDE]
            part_c[to_y, x * 4 + z] = total[:, WIDE:]
            return carry

        lax.fori_loop(0, 16, one, 0, unroll=4)

    def line_copy(i, s, t, device):
        return pltpu.make_async_remote_copy(
            src_ref=s,
            dst_ref=t,
            send_sem=line_send.at[i],
            recv_sem=line_recv.at[i],
            device_id=device,
            device_id_type=MESH,
        )

    around = (2, 1, 3)

    def start_lines(to_y):
        rows = pl.ds(to_y * 4, 4)
        for d in around:
            y = (my_y + d) % 4

            @pl.when(y == to_y)
            def _():
                line_copy(
                    2, part_c.at[to_y], line_c.at[d - 1], at(to_y, my_x, my_z, my_c)
                ).start()

        for d in around:
            x, z = (my_x + d) % 4, (my_z + d) % 4
            to_x, to_z = at(my_y, x, my_z, my_c), at(my_y, my_x, z, my_c)
            line_copy(0, part_a.at[x, rows], line_a.at[d - 1, rows], to_x).start()
            line_copy(1, part_b.at[z, rows], line_b.at[d - 1, rows], to_z).start()

    for to_y in (0, 1):
        core_copy(to_y).wait()
        add_core(to_y)
        start_lines(to_y)

    grad_item = permute(onehots[5], arrived(5))
    delta_item = factors[0] * grad_item
    low_item0 = delta_item.astype(BF16)
    for q in range(4):
        rows = slice(q * 256, (q + 1) * 256)
        blocks = slice(32 + q * 8, 32 + (q + 1) * 8)
        weight_acc[blocks] += rows_dot(prev_t_here[rows], low_item0).reshape(8, 2, 16, D)
        if q % 2 == 1:
            core_copy(2 + q // 2).start()
    src[7] = low_item0.astype(F32)
    start_exchange(7)
    add_vectors(2, delta_item, gap0h)
    vec_to_core = pltpu.make_async_remote_copy(
        src_ref=vec,
        dst_ref=vec_core,
        send_sem=core_send.at[4],
        recv_sem=core_recv.at[4],
        device_id=sibling,
        device_id_type=MESH,
    )
    vec_to_core.start()
    grads_item[...] = grad_item
    for to_y in (2, 3):
        core_copy(to_y).wait()
        add_core(to_y)
        start_lines(to_y)
    vec_to_core.wait()
    vec_acc[0] = vec[...] + vec_core[...]
    for d in around:
        to_x = at(my_y, (my_x + d) % 4, my_z, my_c)
        line_copy(3, vec_acc.at[0], vec_line.at[d - 1], to_x).start()

    low_user0h = arrived(6).astype(BF16)
    new_item = rows_dot_t(low_user0h, v_uw[D : 2 * D]) + rows_dot_t(low_item0, v_iw[0:D])
    v_item_out[...] = permute(
        scatter_matrix(v_islot, 0), jnp.where(live0h > 0.0, new_item, grads_item[...])
    )
    item_done = pltpu.make_async_copy(v_item_out, item_out, out_sem.at[0])
    item_done.start()

    line_refs = [line_a, line_b, line_c, vec_line]
    for i, ref in enumerate(line_refs):
        wait_bytes(ref, line_recv.at[i])
    sum_a[...] = part_a[my_x] + line_a[0] + line_a[1] + line_a[2]
    sum_b[...] = part_b[my_z] + line_b[0] + line_b[1] + line_b[2]
    sum_c[...] = part_c[my_y] + line_c[0] + line_c[1] + line_c[2]
    vec_acc[1] = vec_acc[0] + vec_line[0] + vec_line[1] + vec_line[2]

    def start_plane(n, carry):
        d, e = n // 4, n % 4
        ay, az = (my_y + d) % 4, (my_z + e) % 4
        by, bx = (my_y + d) % 4, (my_x + e) % 4
        cx, cz = (my_x + d) % 4, (my_z + e) % 4
        specs = [
            (sum_a.at[ay * 4 + az], plane_a.at[n - 1], at(ay, my_x, az, my_c)),
            (sum_b.at[by * 4 + bx], plane_b.at[n - 1], at(by, bx, my_z, my_c)),
            (sum_c.at[cx * 4 + cz], plane_c.at[n - 1], at(my_y, cx, cz, my_c)),
            (vec_acc.at[1], vec_plane.at[n - 1], at(ay, my_x, az, my_c)),
        ]
        for i, (s, t, device) in enumerate(specs):
            pltpu.make_async_remote_copy(
                src_ref=s,
                dst_ref=t,
                send_sem=plane_send.at[i],
                recv_sem=plane_recv.at[i],
                device_id=device,
                device_id_type=MESH,
            ).start()
        return carry

    lax.fori_loop(1, 16, start_plane, 0)

    low_item0s = arrived(7).astype(BF16)
    new_user = base_user[...] + rows_dot_t(low_item0s, v_iw[D : 2 * D])
    v_user_out[...] = permute(
        scatter_matrix(v_uslot, 0), jnp.where(live0 > 0.0, new_user, grads_user[...])
    )
    user_done = pltpu.make_async_copy(v_user_out, user_out, out_sem.at[1])
    user_done.start()

    planes = [plane_a, plane_b, plane_c, vec_plane]
    for i, ref in enumerate(planes):
        wait_bytes(ref, plane_recv.at[i])

    def total(own_part, ref):
        result = own_part
        for n in range(15):
            result = result + ref[n]
        return result * scale

    weight_out[0:8, 0:WIDE] = total(sum_a[my_y * 4 + my_z], plane_a)
    weight_out[8:16, 0:WIDE] = total(sum_b[my_y * 4 + my_x], plane_b)
    weight_out[:, WIDE:] = total(sum_c[my_x * 4 + my_z], plane_c)
    vector_out[...] = total(vec_acc[1], vec_plane)[0:4]

    item_done.wait()
    user_done.wait()
    for i in range(10):
        sent(i)
    sent_aux()
    for i, ref in enumerate(line_refs):
        wait_bytes(ref, line_send.at[i])
    for i, ref in enumerate(planes):
        wait_bytes(ref, plane_send.at[i])


def hand_over(a, b, c, d, a_out, b_out, c_out, d_out):
    a_out[...] = a[...]
    b_out[...] = b[...]
    c_out[...] = c[...]
    d_out[...] = d[...]


def per_device(*arrays):
    user_prev = arrays[4]
    batches = user_prev.shape[0]
    scale = 1.0 / math.sqrt(batches * OWNERS * ROWS)
    any_spec = pl.BlockSpec(memory_space=pl.ANY)
    vmem_spec = pl.BlockSpec(memory_space=pltpu.VMEM)
    vmem = pltpu.VMEM
    dma = pltpu.SemaphoreType.DMA
    scratch = [vmem(a.shape, a.dtype) for a in arrays]
    scratch += [
        dma((11,)),
        vmem((10, ROWS, D), F32),
        vmem((10, ROWS, D), F32),
        dma((10,)),
        dma((10,)),
        vmem((ROWS, AUX), F32),
        vmem((ROWS, AUX), F32),
        dma,
        dma,
        vmem((ROWS, 1, D), F32),
        vmem((ROWS, 1, AUX), F32),
        vmem((6, ROWS, ROWS), BF16),
        vmem((3, ROWS, D), F32),
        vmem((2 * D, 4 * ROWS), BF16),
        vmem((2 * D, ROWS), BF16),
        vmem((4 * ROWS, D), BF16),
        vmem((4 * ROWS, D), BF16),
        vmem((ROWS, D), F32),
        vmem((ROWS, D), F32),
        vmem((ROWS, D), F32),
        vmem((ROWS, D), F32),
        vmem((8, D), F32),
        vmem((8, D), F32),
        vmem((3, 8, D), F32),
        vmem((15, 8, D), F32),
        vmem((2, 8, D), F32),
        vmem((64, 2, 16, D), F32),
        vmem((64, 16, D), F32),
        vmem((4, 16, 8, WIDE), F32),
        vmem((4, 16, 8, WIDE), F32),
        vmem((4, 16, 16, D - WIDE), F32),
        vmem((3, 16, 8, WIDE), F32),
        vmem((3, 16, 8, WIDE), F32),
        vmem((3, 16, 16, D - WIDE), F32),
        vmem((16, 8, WIDE), F32),
        vmem((16, 8, WIDE), F32),
        vmem((16, 16, D - WIDE), F32),
        vmem((15, 8, WIDE), F32),
        vmem((15, 8, WIDE), F32),
        vmem((15, 16, D - WIDE), F32),
        dma((5,)),
        dma((5,)),
        dma((4,)),
        dma((4,)),
        dma((4,)),
        dma((4,)),
        vmem((ROWS, D), F32),
        vmem((ROWS, D), F32),
        dma((2,)),
    ]
    outputs = pl.pallas_call(
        functools.partial(kernel, scale),
        out_shape=(
            jax.ShapeDtypeStruct((ROWS, D), F32),
            jax.ShapeDtypeStruct((ROWS, D), F32),
            jax.ShapeDtypeStruct((16, D), F32),
            jax.ShapeDtypeStruct((4, D), F32),
        ),
        in_specs=[any_spec] * 11,
        out_specs=(any_spec, any_spec, vmem_spec, vmem_spec),
        scratch_shapes=scratch,
        compiler_params=pltpu.CompilerParams(
            collective_id=0, has_side_effects=True, vmem_limit_bytes=56 * 2**20
        ),
        cost_estimate=pl.CostEstimate(
            flops=12_000_000_000, bytes_accessed=5_000_000, transcendentals=600_000
        ),
    )(*arrays)
    return pl.pallas_call(
        hand_over,
        out_shape=tuple(jax.ShapeDtypeStruct(a.shape, a.dtype) for a in outputs),
        in_specs=[vmem_spec] * 4,
        out_specs=(vmem_spec,) * 4,
    )(*outputs)


def solution(mesh):
    both = ("grp", "own")
    in_specs = (
        P(None, both, None),
        P(None, both, None),
        P(None, both, None),
        P(None, both),
        P(None, both, None),
        P(None, both, None),
        P(both, None),
        P(both, None),
        P(),
        P(),
        P(),
    )
    out_specs = (P(both, None), P(both, None), P(both, None), P())
    return jax.shard_map(
        per_device, mesh=mesh, in_specs=in_specs, out_specs=out_specs, check_vma=False
    )
```

time: 88.7 us -> 77.8 us (0.88)
  Pallas kernels: 84.1 us -> 77 us
  local copies, waits for them, and re-layouts: 3.78 us -> 0 us
    pallas_call x1, Pallas kernels: 84.1 us -> 75.1 us  [per_device(): pl.pallas_call(functools.partial(kernel, scale), out_shape=(jax.ShapeDtyp...]
    unnamed x10 -> x0, local copies, waits for them, and re-layouts: 3.78 us -> none
    pallas_call x0 -> x1, Pallas kernels: none -> 1.85 us  [per_device(): pl.pallas_call(hand_over, out_shape=tuple((jax.ShapeDtypeStruct(a.shape,...]
where the time goes in v2:
time: 77.8 us; the launch traced here: 77.6 us
  Pallas kernels  77 us (99%)
    pallas_call x1, Pallas kernels, per_device(): pl.pallas_call(functools.partial(kernel, scale), out_shape=(jax.ShapeDtyp...  75.1 us
    pallas_call x1, Pallas kernels, per_device(): pl.pallas_call(hand_over, out_shape=tuple((jax.ShapeDtypeStruct(a.shape,...  1.85 us

profile of v2, /device:TPU:0, one launch (start us, length us, event | category | flops | bytes accessed | tf_op | source)
XLA Modules:
  0.0 77.6 jit_solution(14012193429750109228)
XLA Ops:
  0.6 75.1 %shard_map.138 = (f32[128,512]{1,0:T(8,128)}, f32[128,512]{1,0:T(8,128)}, f32[16,512]{1,0:T(8,128)}, f32[4,512]{1,0:T(4,128)}) custom-call(s32[4,1,128]{2,1,0:T(1,128)} %user_slot.1, s32[4,1,128]{2,1,0:T(1,128)} %item_slot.1, s32[4,1,128]{2,1,0:T(1,128)} %counts.1, f32[4,128]{1,0:T(4,128)} %gaps_in.1, bf16[4,128,512]{2,1,0:T(8,128)(2,1)} %user_prev.1, ...), custom_call_target="tpu_custom_call" | custom-call | flops 12000000000 | bytes 5000000 | tf_op jit(solution)/shard_map/pallas_call | solution.py:626
  75.8 1.8 %shard_map.139 = (f32[128,512]{1,0:T(8,128)}, f32[128,512]{1,0:T(8,128)}, f32[16,512]{1,0:T(8,128)}, f32[4,512]{1,0:T(4,128)}) custom-call(f32[128,512]{1,0:T(8,128)} %get-tuple-element.8.a, f32[128,512]{1,0:T(8,128)} %get-tuple-element.9.b, f32[16,512]{1,0:T(8,128)} %get-tuple-element.10.c, f32[4,512]{1,0:T(4,128)} %get-tuple-element.11.d), custom_call_target="tpu_custom_call" | custom-call | tf_op jit(solution)/shard_map/pallas_call | solution.py:644

commit v3 on v2

--- a/solution.py
+++ b/solution.py
@@ -94,8 +94,9 @@
     vec,
     vec_core,
     vec_line,
-    vec_plane,
     vec_acc,
+    vec_send,
+    vec_recv,
     weight_acc,
     core_in,
     part_a,
@@ -175,7 +176,7 @@
             ).start()
             return carry
 
-        lax.fori_loop(1, OWNERS, one, 0)
+        lax.fori_loop(1, OWNERS, one, 0, unroll=2)
         target[pl.ds(me, 1)] = source[pl.ds(me, 1)]
 
     def wait_bytes(ref, sem):
@@ -266,6 +267,8 @@
     u2, i2, gap2, live2 = saved(2)
     src[8] = jnp.where(live2 > 0.0, item_factor(u2, i2, gap2), -1.0)
     start_exchange(8)
+    src[9] = v_uprev[0].astype(F32)
+    start_exchange(9)
 
     u3, i3, gap3, live3 = saved(3)
     factors[0] = live3 * item_factor(u3, i3, gap3)
@@ -307,8 +310,6 @@
     keep_transposed(3, u3, i3)
     keep_transposed(2, u2, i2)
 
-    src[9] = v_uprev[0].astype(F32)
-    start_exchange(9)
 
     factor = arrived(8)
     grad_item = permute(onehots[1], arrived(1))
@@ -391,6 +392,7 @@
             prev_t[rows, ROWS:], low_item_all[ROWS:]
         ).reshape(8, 2, 16, D)
 
+
     start_exchange(6)
 
     wait_bytes(dummy.at[pl.ds(0, OWNERS - 1)], a2a_recv.at[9])
@@ -428,6 +430,29 @@
 
     around = (2, 1, 3)
 
+    def start_vec_line(axis):
+        for d in around:
+            x, y, z = (my_x + d) % 4, (my_y + d) % 4, (my_z + d) % 4
+            device = [
+                at(my_y, x, my_z, my_c),
+                at(y, my_x, my_z, my_c),
+                at(my_y, my_x, z, my_c),
+            ][axis]
+            pltpu.make_async_remote_copy(
+                src_ref=vec_acc.at[axis],
+                dst_ref=vec_line.at[axis, d - 1],
+                send_sem=vec_send.at[axis],
+                recv_sem=vec_recv.at[axis],
+                device_id=device,
+                device_id_type=MESH,
+            ).start()
+
+    def add_vec_line(axis):
+        wait_bytes(vec_line.at[axis], vec_recv.at[axis])
+        vec_acc[axis + 1] = (
+            vec_acc[axis] + vec_line[axis, 0] + vec_line[axis, 1] + vec_line[axis, 2]
+        )
+
     def start_lines(to_y):
         rows = pl.ds(to_y * 4, 4)
         for d in around:
@@ -460,7 +485,6 @@
         if q % 2 == 1:
             core_copy(2 + q // 2).start()
     src[7] = low_item0.astype(F32)
-    start_exchange(7)
     add_vectors(2, delta_item, gap0h)
     vec_to_core = pltpu.make_async_remote_copy(
         src_ref=vec,
@@ -472,31 +496,25 @@
     )
     vec_to_core.start()
     grads_item[...] = grad_item
+    vec_to_core.wait()
+    vec_acc[0] = vec[...] + vec_core[...]
+    start_vec_line(0)
     for to_y in (2, 3):
         core_copy(to_y).wait()
         add_core(to_y)
         start_lines(to_y)
-    vec_to_core.wait()
-    vec_acc[0] = vec[...] + vec_core[...]
-    for d in around:
-        to_x = at(my_y, (my_x + d) % 4, my_z, my_c)
-        line_copy(3, vec_acc.at[0], vec_line.at[d - 1], to_x).start()
-
-    low_user0h = arrived(6).astype(BF16)
-    new_item = rows_dot_t(low_user0h, v_uw[D : 2 * D]) + rows_dot_t(low_item0, v_iw[0:D])
-    v_item_out[...] = permute(
-        scatter_matrix(v_islot, 0), jnp.where(live0h > 0.0, new_item, grads_item[...])
-    )
-    item_done = pltpu.make_async_copy(v_item_out, item_out, out_sem.at[0])
-    item_done.start()
-
-    line_refs = [line_a, line_b, line_c, vec_line]
+    start_exchange(7)
+
+    for axis in (1, 2):
+        add_vec_line(axis - 1)
+        start_vec_line(axis)
+
+    line_refs = [line_a, line_b, line_c]
     for i, ref in enumerate(line_refs):
         wait_bytes(ref, line_recv.at[i])
     sum_a[...] = part_a[my_x] + line_a[0] + line_a[1] + line_a[2]
     sum_b[...] = part_b[my_z] + line_b[0] + line_b[1] + line_b[2]
     sum_c[...] = part_c[my_y] + line_c[0] + line_c[1] + line_c[2]
-    vec_acc[1] = vec_acc[0] + vec_line[0] + vec_line[1] + vec_line[2]
 
     def start_plane(n, carry):
         d, e = n // 4, n % 4
@@ -507,7 +525,6 @@
             (sum_a.at[ay * 4 + az], plane_a.at[n - 1], at(ay, my_x, az, my_c)),
             (sum_b.at[by * 4 + bx], plane_b.at[n - 1], at(by, bx, my_z, my_c)),
             (sum_c.at[cx * 4 + cz], plane_c.at[n - 1], at(my_y, cx, cz, my_c)),
-            (vec_acc.at[1], vec_plane.at[n - 1], at(ay, my_x, az, my_c)),
         ]
         for i, (s, t, device) in enumerate(specs):
             pltpu.make_async_remote_copy(
@@ -530,7 +547,18 @@
     user_done = pltpu.make_async_copy(v_user_out, user_out, out_sem.at[1])
     user_done.start()
 
-    planes = [plane_a, plane_b, plane_c, vec_plane]
+    add_vec_line(2)
+    vector_out[...] = vec_acc[3, 0:4] * scale
+
+    low_user0h = arrived(6).astype(BF16)
+    new_item = rows_dot_t(low_user0h, v_uw[D : 2 * D]) + rows_dot_t(low_item0, v_iw[0:D])
+    v_item_out[...] = permute(
+        scatter_matrix(v_islot, 0), jnp.where(live0h > 0.0, new_item, grads_item[...])
+    )
+    item_done = pltpu.make_async_copy(v_item_out, item_out, out_sem.at[0])
+    item_done.start()
+
+    planes = [plane_a, plane_b, plane_c]
     for i, ref in enumerate(planes):
         wait_bytes(ref, plane_recv.at[i])
 
@@ -543,7 +571,6 @@
     weight_out[0:8, 0:WIDE] = total(sum_a[my_y * 4 + my_z], plane_a)
     weight_out[8:16, 0:WIDE] = total(sum_b[my_y * 4 + my_x], plane_b)
     weight_out[:, WIDE:] = total(sum_c[my_x * 4 + my_z], plane_c)
-    vector_out[...] = total(vec_acc[1], vec_plane)[0:4]
 
     item_done.wait()
     user_done.wait()
@@ -552,6 +579,8 @@
     sent_aux()
     for i, ref in enumerate(line_refs):
         wait_bytes(ref, line_send.at[i])
+    for i in range(3):
+        wait_bytes(vec_line.at[i], vec_send.at[i])
     for i, ref in enumerate(planes):
         wait_bytes(ref, plane_send.at[i])
 
@@ -596,9 +625,10 @@
         vmem((ROWS, D), F32),
         vmem((8, D), F32),
         vmem((8, D), F32),
-        vmem((3, 8, D), F32),
-        vmem((15, 8, D), F32),
-        vmem((2, 8, D), F32),
+        vmem((3, 3, 8, D), F32),
+        vmem((4, 8, D), F32),
+        dma((3,)),
+        dma((3,)),
         vmem((64, 2, 16, D), F32),
         vmem((64, 16, D), F32),
         vmem((4, 16, 8, WIDE), F32),
@@ -615,10 +645,10 @@
         vmem((15, 16, D - WIDE), F32),
         dma((5,)),
         dma((5,)),
-        dma((4,)),
-        dma((4,)),
-        dma((4,)),
-        dma((4,)),
+        dma((3,)),
+        dma((3,)),
+        dma((3,)),
+        dma((3,)),
         vmem((ROWS, D), F32),
         vmem((ROWS, D), F32),
         dma((2,)),

time: 77.8 us -> 72.5 us (0.932)
  Pallas kernels: 77 us -> 71.7 us
    pallas_call x1, Pallas kernels: 75.1 us -> 69.8 us  [per_device(): pl.pallas_call(functools.partial(kernel, scale), out_shape=(jax.ShapeDtyp...]
where the time goes in v3:
time: 72.5 us; the launch traced here: 72.3 us
  Pallas kernels  71.7 us (99%)
    pallas_call x1, Pallas kernels, per_device(): pl.pallas_call(functools.partial(kernel, scale), out_shape=(jax.ShapeDtyp...  69.8 us
    pallas_call x1, Pallas kernels, per_device(): pl.pallas_call(hand_over, out_shape=tuple((jax.ShapeDtypeStruct(a.shape,...  1.85 us

profile of v3, /device:TPU:0, one launch (start us, length us, event | category | flops | bytes accessed | tf_op | source)
XLA Modules:
  0.0 72.3 jit_solution(13585063250449292835)
XLA Ops:
  0.6 69.8 %shard_map.138 = (f32[128,512]{1,0:T(8,128)}, f32[128,512]{1,0:T(8,128)}, f32[16,512]{1,0:T(8,128)}, f32[4,512]{1,0:T(4,128)}) custom-call(s32[4,1,128]{2,1,0:T(1,128)} %user_slot.1, s32[4,1,128]{2,1,0:T(1,128)} %item_slot.1, s32[4,1,128]{2,1,0:T(1,128)} %counts.1, f32[4,128]{1,0:T(4,128)} %gaps_in.1, bf16[4,128,512]{2,1,0:T(8,128)(2,1)} %user_prev.1, ...), custom_call_target="tpu_custom_call" | custom-call | flops 12000000000 | bytes 5000000 | tf_op jit(solution)/shard_map/pallas_call | solution.py:656
  70.5 1.8 %shard_map.139 = (f32[128,512]{1,0:T(8,128)}, f32[128,512]{1,0:T(8,128)}, f32[16,512]{1,0:T(8,128)}, f32[4,512]{1,0:T(4,128)}) custom-call(f32[128,512]{1,0:T(8,128)} %get-tuple-element.8.a, f32[128,512]{1,0:T(8,128)} %get-tuple-element.9.b, f32[16,512]{1,0:T(8,128)} %get-tuple-element.10.c, f32[4,512]{1,0:T(4,128)} %get-tuple-element.11.d), custom_call_target="tpu_custom_call" | custom-call | tf_op jit(solution)/shard_map/pallas_call | solution.py:674

commit v4 on v3

--- a/solution.py
+++ b/solution.py
@@ -509,6 +509,14 @@
         add_vec_line(axis - 1)
         start_vec_line(axis)
 
+    low_user0h = arrived(6).astype(BF16)
+    new_item = rows_dot_t(low_user0h, v_uw[D : 2 * D]) + rows_dot_t(low_item0, v_iw[0:D])
+    v_item_out[...] = permute(
+        scatter_matrix(v_islot, 0), jnp.where(live0h > 0.0, new_item, grads_item[...])
+    )
+    item_done = pltpu.make_async_copy(v_item_out, item_out, out_sem.at[0])
+    item_done.start()
+
     line_refs = [line_a, line_b, line_c]
     for i, ref in enumerate(line_refs):
         wait_bytes(ref, line_recv.at[i])
@@ -549,14 +557,6 @@
 
     add_vec_line(2)
     vector_out[...] = vec_acc[3, 0:4] * scale
-
-    low_user0h = arrived(6).astype(BF16)
-    new_item = rows_dot_t(low_user0h, v_uw[D : 2 * D]) + rows_dot_t(low_item0, v_iw[0:D])
-    v_item_out[...] = permute(
-        scatter_matrix(v_islot, 0), jnp.where(live0h > 0.0, new_item, grads_item[...])
-    )
-    item_done = pltpu.make_async_copy(v_item_out, item_out, out_sem.at[0])
-    item_done.start()
 
     planes = [plane_a, plane_b, plane_c]
     for i, ref in enumerate(planes):

time: 72.5 us -> 73.2 us (level)
  no operation moved by 1% of the time
where the time goes in v4:
time: 73.2 us; the launch traced here: 73 us
  Pallas kernels  72.4 us (99%)
    pallas_call x1, Pallas kernels, per_device(): pl.pallas_call(functools.partial(kernel, scale), out_shape=(jax.ShapeDtyp...  70.5 us
    pallas_call x1, Pallas kernels, per_device(): pl.pallas_call(hand_over, out_shape=tuple((jax.ShapeDtypeStruct(a.shape,...  1.85 us

profile of v4, /device:TPU:0, one launch (start us, length us, event | category | flops | bytes accessed | tf_op | source)
XLA Modules:
  0.0 73.0 jit_solution(732616575105466202)
XLA Ops:
  0.6 70.5 %shard_map.138 = (f32[128,512]{1,0:T(8,128)}, f32[128,512]{1,0:T(8,128)}, f32[16,512]{1,0:T(8,128)}, f32[4,512]{1,0:T(4,128)}) custom-call(s32[4,1,128]{2,1,0:T(1,128)} %user_slot.1, s32[4,1,128]{2,1,0:T(1,128)} %item_slot.1, s32[4,1,128]{2,1,0:T(1,128)} %counts.1, f32[4,128]{1,0:T(4,128)} %gaps_in.1, bf16[4,128,512]{2,1,0:T(8,128)(2,1)} %user_prev.1, ...), custom_call_target="tpu_custom_call" | custom-call | flops 12000000000 | bytes 5000000 | tf_op jit(solution)/shard_map/pallas_call | solution.py:656
  71.2 1.8 %shard_map.139 = (f32[128,512]{1,0:T(8,128)}, f32[128,512]{1,0:T(8,128)}, f32[16,512]{1,0:T(8,128)}, f32[4,512]{1,0:T(4,128)}) custom-call(f32[128,512]{1,0:T(8,128)} %get-tuple-element.8.a, f32[128,512]{1,0:T(8,128)} %get-tuple-element.9.b, f32[16,512]{1,0:T(8,128)} %get-tuple-element.10.c, f32[4,512]{1,0:T(4,128)} %get-tuple-element.11.d), custom_call_target="tpu_custom_call" | custom-call | tf_op jit(solution)/shard_map/pallas_call | solution.py:674
